TPU v7x, 256 devices: a whole 4x4x8 slice. The times are simulated.
256 devices in a mesh: wide: 16 (over y_lo, x, core), narrow: 16 (over z, y_hi).
Axes of the slice: x: 4, y: 4 (y_hi: 2, y_lo: 2; y = y_hi * 2 + y_lo), z: 8, core: 2. Of those that a mesh axis runs over, the one named last changes fastest.
Arguments:
- batch_index: int32 [1024], P('narrow'), may hold values from 0 to 255
- train_features: float32 [4096, 1024], P('narrow'), may hold values from -6 to 6
- train_labels: float32 [4096, 1000], P('narrow'), may hold values from -12 to 12
- centers: float32 [65536, 1024], P(('wide', 'narrow')), may hold values from -6 to 6
- weights: float32 [65536, 1000], P(('wide', 'narrow')), may hold values from -6 to 6
Outputs:
- new_weights: float32 [65536, 1000], P(('wide', 'narrow'))
- residual: float32 [1024, 1000], P('narrow')
Inputs may be any that keep to these rules, and one draw needn't show every extreme that they name: `batch_index`: entry i names a row of the training shard held by narrow index i // 64.
All inputs are finite; a program needn't handle non-finite values.
Results may differ from a plain program's by a relative error of at most 0.0001.
Values sent between devices are 32-bit elements; how exact they have to be, the bound alone decides.
No kernel may reach another device: no remote copies, remote signals or barrier semaphores. Data moves between devices by JAX's collectives and lax.ppermute only.
A program may use at most 64 MiB of HBM per device.

v0:
```python
import math
import jax
import jax.numpy as jnp
from jax import lax
from jax.sharding import Mesh
from jax.sharding import PartitionSpec as P

NARROW = ("narrow_0", "narrow_1")
WIDE_NARROW = ("wide", "narrow_0", "narrow_1")
step_size = 1.0


def gather_axes(array, axes, dim):
    for axis in reversed(axes):
        array = lax.all_gather(array, axis, axis=dim, tiled=True)
    return array


def per_device(batch_index, train_features, train_labels, centers, weights):
    block = batch_index.shape[0]
    rows = jnp.take(train_features, batch_index, axis=0)
    targets = jnp.take(train_labels, batch_index, axis=0)
    features = centers.shape[1]
    center_sq = jnp.sum(centers * centers, axis=1)
    count = centers.shape[0] * lax.axis_size("wide") * lax.axis_size(NARROW)
    scale = 1.0 / math.sqrt(count)
    piece = gather_axes(rows, NARROW, 0)
    inner = jnp.dot(
        piece, centers.T, precision=lax.Precision.HIGHEST, preferred_element_type=jnp.float32
    )
    piece_sq = jnp.sum(piece * piece, axis=1)
    kernel = jnp.exp(
        (2.0 * features - piece_sq[:, None] - center_sq[None, :] + 2.0 * inner) / 128.0
    )
    batch = kernel.shape[0]
    partial_value = jnp.dot(
        kernel, weights, precision=lax.Precision.HIGHEST, preferred_element_type=jnp.float32
    )
    owner = jnp.where(lax.axis_index("wide") == 0, 1.0, 0.0).astype(jnp.float32)
    placed = lax.dynamic_update_slice_in_dim(
        jnp.zeros((batch, targets.shape[1]), jnp.float32),
        targets * owner,
        lax.axis_index(NARROW) * block,
        0,
    )
    resid_all = lax.psum(partial_value * scale - placed, WIDE_NARROW)
    residual = lax.dynamic_slice_in_dim(resid_all, lax.axis_index(NARROW) * block, block, 0)
    delta = lax.dot_general(
        kernel,
        resid_all,
        (((0,), (0,)), ((), ())),
        precision=lax.Precision.HIGHEST,
        preferred_element_type=jnp.float32,
    )
    new_weights = weights - step_size / batch * delta
    return (new_weights, residual)


def solution(mesh):
    split = Mesh(mesh.devices.reshape(mesh.shape["wide"], 8, 2), ("wide", "narrow_0", "narrow_1"))
    placed = (
        P(NARROW),
        P(NARROW, None),
        P(NARROW, None),
        P(WIDE_NARROW, None),
        P(WIDE_NARROW, None),
    )
    return jax.shard_map(
        per_device,
        mesh=split,
        in_specs=placed,
        out_specs=(P(WIDE_NARROW, None), P(NARROW, None)),
        check_vma=False,
    )
```

profile of v0, /device:TPU:2, one launch (start us, length us, event | category | flops | bytes accessed | tf_op | source)
XLA Modules:
  0.0 375.1 jit_solution(9159140242311068464)
XLA Ops:
  7.2 0.0 all-gather.2.cloned.1.call-start
  7.2 0.8 compare_select_fusion
  8.0 0.7 compare_and_fusion
  8.7 0.7 gather_fusion
  9.4 0.1 broadcast_select_fusion
  9.5 10.3 %all_gather.6 = f32[128,1024]{1,0:T(8,128)} all-gather(f32[64,1024]{1,0:T(8,128)S(1)} %broadcast_select_fusion), channel_id=1, replica_groups=mesh['wide'=16,'narrow_0'=8,'narrow_1'=2] {'narrow_1'}, dimensions={0}, use_global_device_ids=true | all-gather | bytes 786432 | tf_op jit(solution)/shard_map/all_gather | solution.py:15
  19.8 0.0 all-gather.2.cloned.1.call-update
  19.8 0.0 all-reduce.2.cloned.1.call-start
  19.9 0.3 copy.7
  20.3 0.7 gather_fusion.1
  21.0 0.2 copy.8
  21.2 2.5 broadcast_in_dim.30
  23.7 3.5 dynamic_update_slice.3
  27.1 0.1 multiply_reduce_fusion.1
  27.3 50.5 %all-gather.2.cloned.1.call-done = f32[1024,1024]{1,0:T(8,128)} async-done(((f32[128,1024]{1,0:T(8,128)}), f32[1024,1024]{1,0:T(8,128)}) %all-gather.2.cloned.1.call-update) | async-done | bytes 4194320 | tf_op jit(solution)/shard_map/all_gather | solution.py:15
  77.8 2.7 multiply_reduce_fusion
  80.5 0.7 copy-done.1
  81.2 3.5 fusion.2
  84.8 5.3 %multiply_subtract_fusion = f32[1024,1000]{0,1:T(8,128)} fusion(f32[1024,1000]{0,1:T(8,128)S(1)} %copy-done.2, f32[1024,256]{1,0:T(8,128)S(1)} %fusion.2, f32[256,1000]{0,1:T(8,128)S(1)} %copy-done.4), kind=kOutput, calls=%fused_computation.3 | convolution fusion | flops 3147776000 | bytes 10264576 | tf_op jit(solution)/shard_map/dot_general | solution.py:36
  90.1 0.0 all-reduce.2.cloned.1.call-update
  90.1 267.7 %all-reduce.2.cloned.1.call-done = f32[1024,1000]{0,1:T(8,128)} async-done(((f32[1024,1000]{0,1:T(8,128)}), f32[1024,1000]{0,1:T(8,128)}) %all-reduce.2.cloned.1.call-update) | async-done | bytes 4096016 | tf_op jit(solution)/shard_map/psum | solution.py:46
  357.8 2.0 constant_dynamic-slice_fusion
  359.8 1.9 copy.9
  361.7 6.5 %fusion.3 = f32[256,1000]{0,1:T(8,128)} fusion(f32[256,1000]{0,1:T(8,128)S(1)} %copy-done.5, f32[1024,256]{1,0:T(8,128)S(1)} %fusion.2, f32[1024,1000]{0,1:T(8,128)} %all-reduce.2.cloned.1.call-done), kind=kOutput, calls=%fused_computation.9 | convolution fusion | flops 3146240000 | bytes 7192576 | tf_op jit(solution)/shard_map/dot_general | solution.py:48
  (16 shorter events, 0.1 us)
Async XLA Ops:
  7.2 1.5 copy-start
  7.2 12.7 %copy-start.6 = (f32[256,1000]{0,1:T(8,128)S(1)}, f32[256,1000]{0,1:T(8,128)}, u32[]{:S(2)}) copy-start(f32[256,1000]{0,1:T(8,128)} %param.7) | copy-start | bytes 3072004
  7.2 70.6 %all-gather.2.cloned.1.call-start = ((), (), s32[]{:S(2)}) async-start(), calls=%async_computation | async-start | bytes 4718592 | tf_op jit(solution)/shard_map/all_gather | solution.py:15
  19.8 337.9 %all-reduce.2.cloned.1.call-start = ((), (), s32[]{:S(2)}) async-start(), calls=%async_computation.1 | async-start | bytes 8192000 | tf_op jit(solution)/shard_map/psum | solution.py:46
  20.3 6.9 %copy-start.3 = (f32[256,1024]{1,0:T(8,128)S(1)}, f32[256,1024]{1,0:T(8,128)}, u32[]{:S(2)}) copy-start(f32[256,1024]{1,0:T(8,128)} %param.8) | copy-start | bytes 3145732
  77.8 3.4 copy-start.1
  80.5 4.3 %copy-start.2 = (f32[1024,1000]{0,1:T(8,128)S(1)}, f32[1024,1000]{0,1:T(8,128)}, u32[]{:S(2)}) copy-start(f32[1024,1000]{0,1:T(8,128)} %dynamic_update_slice.3) | copy-start | bytes 12288004
  80.5 4.3 %copy-start.4 = (f32[256,1000]{0,1:T(8,128)S(1)}, f32[256,1000]{0,1:T(8,128)}, u32[]{:S(2)}) copy-start(f32[256,1000]{0,1:T(8,128)} %param.9) | copy-start | bytes 3072004
  90.1 271.6 %copy-start.5 = (f32[256,1000]{0,1:T(8,128)S(1)}, f32[256,1000]{0,1:T(8,128)}, u32[]{:S(2)}) copy-start(f32[256,1000]{0,1:T(8,128)} %param.9) | copy-start | bytes 3072004
Sparse Core Ops, SparseCore 0:
  20.0 57.7 all-gather.1
  90.2 267.4 all-reduce.1
where the time goes:
time: 375 us
  waiting for transfers between devices  318 us (85%)
  matrix products  15.3 us (4%)
  between operations  14.2 us (4%)
  local copies, waits for them, and re-layouts  12.5 us (3%)
  blocking collectives  10.3 us (3%)
  other arithmetic  4.42 us (1%)
    psum x1, waiting for transfers between devices, per_device(): resid_all = lax.psum(partial_value * scale - placed, WIDE_NARROW)  268 us
    all_gather x1, waiting for transfers between devices, gather_axes(): array = lax.all_gather(array, axis, axis=dim, tiled=True)  50.5 us
    all_gather x1, blocking collectives, gather_axes(): array = lax.all_gather(array, axis, axis=dim, tiled=True)  10.3 us
  transfers between devices with their start and end apart: 2, of which 2 were waited for; matrix products, arithmetic and copies ran while one was open for 2% of the time, Pallas kernels for 0%

commit v1 on v0

--- a/solution.py
+++ b/solution.py
@@ -43,7 +43,7 @@
         lax.axis_index(NARROW) * block,
         0,
     )
-    resid_all = lax.psum(partial_value * scale - placed, WIDE_NARROW)
+    resid_all = lax.psum(lax.psum(partial_value * scale - placed, "wide"), ("narrow_0", "narrow_1"))
     residual = lax.dynamic_slice_in_dim(resid_all, lax.axis_index(NARROW) * block, block, 0)
     delta = lax.dot_general(
         kernel,

time: 375 us -> 451 us (1.20)
  waiting for transfers between devices: 318 us -> 394 us
    psum x1 -> x2, waiting for transfers between devices: 268 us -> 344 us  [the longest x1 214 us: per_device(): lax.psum(lax.psum(partial_value * scale - placed, 'wide'), ('narrow_0', '...]
  transfers between devices with their start and end apart: 2 -> 3, of which waited for: 2 -> 3; matrix products, arithmetic and copies ran while one was open for 2% -> 2% of each run, Pallas kernels for 0% -> 0%
where the time goes in v1:
time: 451 us
  waiting for transfers between devices  394 us (87%)
  matrix products  15.3 us (3%)
  between operations  13.9 us (3%)
  local copies, waits for them, and re-layouts  12.5 us (3%)
  blocking collectives  10.3 us (2%)
    psum x1, waiting for transfers between devices, per_device(): lax.psum(lax.psum(partial_value * scale - placed, 'wide'), ('narrow_0', '...  214 us
    psum x1, waiting for transfers between devices, per_device(): lax.psum(partial_value * scale - placed, 'wide')  129 us
    all_gather x1, waiting for transfers between devices, gather_axes(): array = lax.all_gather(array, axis, axis=dim, tiled=True)  50.5 us
    all_gather x1, blocking collectives, gather_axes(): array = lax.all_gather(array, axis, axis=dim, tiled=True)  10.3 us
  transfers between devices with their start and end apart: 3, of which 3 were waited for; matrix products, arithmetic and copies ran while one was open for 2% of the time, Pallas kernels for 0%

profile of v1, /device:TPU:2, one launch (start us, length us, event | category | flops | bytes accessed | tf_op | source)
XLA Modules:
  0.0 450.8 jit_solution(16162171724074611347)
XLA Ops:
  7.2 0.0 all-gather.2.cloned.1.call-start
  7.2 0.8 compare_select_fusion
  8.0 0.7 compare_and_fusion
  8.7 0.7 gather_fusion
  9.4 0.1 broadcast_select_fusion
  9.5 10.3 %all_gather.6 = f32[128,1024]{1,0:T(8,128)} all-gather(f32[64,1024]{1,0:T(8,128)S(1)} %broadcast_select_fusion), channel_id=1, replica_groups=mesh['wide'=16,'narrow_0'=8,'narrow_1'=2] {'narrow_1'}, dimensions={0}, use_global_device_ids=true | all-gather | bytes 786432 | tf_op jit(solution)/shard_map/all_gather | solution.py:15
  19.8 0.0 all-reduce.3.cloned.1.call-start
  19.9 0.3 copy.7
  20.3 0.7 gather_fusion.1
  21.0 0.2 copy.8
  21.2 2.5 broadcast_in_dim.30
  23.7 3.5 dynamic_update_slice.3
  27.1 0.1 multiply_reduce_fusion.1
  27.3 50.5 %all-gather.2.cloned.1.call-done = f32[1024,1024]{1,0:T(8,128)} async-done(((f32[128,1024]{1,0:T(8,128)}), f32[1024,1024]{1,0:T(8,128)}) %all-gather.2.cloned.1.call-update) | async-done | bytes 4194320 | tf_op jit(solution)/shard_map/all_gather | solution.py:15
  77.8 2.7 multiply_reduce_fusion
  80.5 0.7 copy-done.1
  81.2 3.5 fusion.2
  84.8 5.3 %multiply_subtract_fusion = f32[1024,1000]{0,1:T(8,128)} fusion(f32[1024,1000]{0,1:T(8,128)S(1)} %copy-done.2, f32[1024,256]{1,0:T(8,128)S(1)} %fusion.2, f32[256,1000]{0,1:T(8,128)S(1)} %copy-done.4), kind=kOutput, calls=%fused_computation.3 | convolution fusion | flops 3147776000 | bytes 10264576 | tf_op jit(solution)/shard_map/dot_general | solution.py:36
  90.1 0.0 all-reduce.5.cloned.1.call-start
  90.2 129.3 %all-reduce.3.cloned.1.call-done = f32[1024,1000]{0,1:T(8,128)} async-done(((f32[1024,1000]{0,1:T(8,128)}), f32[1024,1000]{0,1:T(8,128)}) %all-reduce.3.cloned.1.call-update) | async-done | bytes 4096016 | tf_op jit(solution)/shard_map/psum | solution.py:46
  219.5 214.3 %all-reduce.5.cloned.1.call-done = f32[1024,1000]{0,1:T(8,128)} async-done(((f32[1024,1000]{0,1:T(8,128)}), f32[1024,1000]{0,1:T(8,128)}) %all-reduce.5.cloned.1.call-update) | async-done | bytes 4096016 | tf_op jit(solution)/shard_map/psum | solution.py:46
  433.8 2.0 constant_dynamic-slice_fusion
  435.8 1.9 copy.9
  437.8 6.5 %fusion.3 = f32[256,1000]{0,1:T(8,128)} fusion(f32[256,1000]{0,1:T(8,128)S(1)} %copy-done.5, f32[1024,256]{1,0:T(8,128)S(1)} %fusion.2, f32[1024,1000]{0,1:T(8,128)} %all-reduce.5.cloned.1.call-done), kind=kOutput, calls=%fused_computation.9 | convolution fusion | flops 3146240000 | bytes 7192576 | tf_op jit(solution)/shard_map/dot_general | solution.py:48
  (19 shorter events, 0.1 us)
Async XLA Ops:
  7.2 1.5 copy-start
  7.2 12.7 %copy-start.6 = (f32[256,1000]{0,1:T(8,128)S(1)}, f32[256,1000]{0,1:T(8,128)}, u32[]{:S(2)}) copy-start(f32[256,1000]{0,1:T(8,128)} %param.7) | copy-start | bytes 3072004
  7.2 70.6 %all-gather.2.cloned.1.call-start = ((), (), s32[]{:S(2)}) async-start(), calls=%async_computation | async-start | bytes 4718592 | tf_op jit(solution)/shard_map/all_gather | solution.py:15
  19.8 199.6 %all-reduce.3.cloned.1.call-start = ((), (), s32[]{:S(2)}) async-start(), calls=%async_computation.1 | async-start | bytes 8192000 | tf_op jit(solution)/shard_map/psum | solution.py:46
  20.3 6.9 %copy-start.3 = (f32[256,1024]{1,0:T(8,128)S(1)}, f32[256,1024]{1,0:T(8,128)}, u32[]{:S(2)}) copy-start(f32[256,1024]{1,0:T(8,128)} %param.8) | copy-start | bytes 3145732
  77.8 3.4 copy-start.1
  80.5 4.3 copy-start.2
  80.5 4.3 copy-start.4
  90.1 347.7 %copy-start.5 = (f32[256,1000]{0,1:T(8,128)S(1)}, f32[256,1000]{0,1:T(8,128)}, u32[]{:S(2)}) copy-start(f32[256,1000]{0,1:T(8,128)} %param.9) | copy-start | bytes 3072004
  90.1 343.7 %all-reduce.5.cloned.1.call-start = ((), (), s32[]{:S(2)}) async-start(), calls=%async_computation.2 | async-start | bytes 8192000 | tf_op jit(solution)/shard_map/psum | solution.py:46
Sparse Core Ops, SparseCore 0:
  20.0 57.7 all-gather.1
  90.2 129.2 all-reduce.2
  222.2 211.5 all-reduce.4
